TPU v7x, 512 devices: a whole 4x8x8 slice. The times are simulated.
512 devices in a mesh: leaf: 64 (over z_lo, x, y), head: 8 (over z_hi, core).
Axes of the slice: x: 4, y: 8, z: 8 (z_hi: 4, z_lo: 2; z = z_hi * 2 + z_lo), core: 2. Of those that a mesh axis runs over, the one named last changes fastest.
Arguments:
- queries: bfloat16 [8192, 64, 576], P('leaf', 'head'), may hold values from -40 to 40
- leaf_latent: bfloat16 [8192, 576], P('leaf'), may hold values from -4 to 4
- node_latent: bfloat16 [64, 96, 576], P('leaf', 'head'), may hold values from -4 to 4
- grad_out: bfloat16 [8192, 64, 512], P('leaf', 'head'), may hold values from -6 to 6
- leaf_nodes: int32 [128, 3], P('leaf'), may hold values from 0 to 63, as said below
- leaf_lengths: int32 [128], P('leaf'), may hold values from 1 to 64, 5120 in all
Outputs:
- attention: bfloat16 [8192, 64, 512], P('leaf', 'head')
- node_grad: bfloat16 [64, 96, 576], P('leaf', 'head')
- leaf_grad: bfloat16 [8192, 576], P('leaf')
Inputs may be any that keep to these rules, and one draw needn't show every extreme that they name: `leaf_nodes`: each row lists three different nodes: a root, one of its children and one of that child's children. Every node has one level and one parent; which nodes are used and how often varies.
All inputs are finite; a program needn't handle non-finite values. No bound on the sum of `leaf_lengths` on one device may be relied on, other than what follows from the above.
Results may differ from a plain program's by a relative error of at most 0.0095.
Values may be sent and summed in bfloat16 or wider, within the bound.
A program may use at most 64 MiB of HBM per device.

v0:
```python
import jax
import jax.numpy as jnp
from jax import lax
from jax.sharding import PartitionSpec as P

LAT = 512
NODE_ROWS = 96


score_scale = 192.0 ** (-0.5)


def from_everyone(shard, axis):
    devices = lax.axis_size(axis)
    return lax.all_to_all(
        jnp.broadcast_to(shard[None], (devices, *shard.shape)), axis, 0, 0, tiled=True
    )


def in_order(pieces, dim):
    pieces = jnp.moveaxis(pieces, 0, dim)
    lengths = pieces.shape
    return pieces.reshape(*lengths[:dim], lengths[dim] * lengths[dim + 1], *lengths[dim + 2 :])


def gather_directly(shard, axis, dim):
    pieces = from_everyone(shard, axis)
    return in_order(pieces, dim)


def cut_along(shard, dim, devices):
    before, after = (shard.shape[:dim], shard.shape[dim + 1 :])
    return jnp.moveaxis(shard.reshape(*before, devices, -1, *after), dim, 0)


def sum_at_owner(shard, axis, dim):
    pieces = cut_along(shard, dim, lax.axis_size(axis))
    arrived = lax.all_to_all(pieces, axis, split_axis=0, concat_axis=0, tiled=True)
    return arrived.astype(jnp.float32).sum(axis=0)


def body(queries, leaf_latent, node_latent, grad_out, leaf_nodes, leaf_lengths):
    rows, heads, width = queries.shape
    leaves = leaf_nodes.shape[0]
    leaf_rows = rows // leaves
    slices = gather_directly(node_latent, "leaf", 0)
    total_nodes = slices.shape[0]
    node_ids = leaf_nodes.reshape(-1)
    picker = (node_ids[:, None] == jnp.arange(total_nodes, dtype=jnp.int32)[None, :]).astype(
        jnp.bfloat16
    )
    chosen = jnp.dot(picker, slices.reshape(total_nodes, -1), preferred_element_type=jnp.float32)
    chosen = chosen.astype(jnp.bfloat16).reshape(leaves * 3, -1, width)
    whole_nodes = gather_directly(chosen, "head", 1)
    node_keys = whole_nodes.reshape(leaves, 3 * NODE_ROWS, width)
    keys = jnp.concatenate([node_keys, leaf_latent.reshape(leaves, leaf_rows, width)], axis=1)
    values = keys[:, :, :LAT]
    total_keys = keys.shape[1]
    query = queries.reshape(leaves, leaf_rows * heads, width)
    row_of = jnp.arange(leaf_rows * heads, dtype=jnp.int32) // heads
    key_index = jnp.arange(total_keys, dtype=jnp.int32)
    visible = (key_index[None, :] < 3 * NODE_ROWS) | (
        key_index[None, :] - 3 * NODE_ROWS <= row_of[:, None]
    )
    live = (row_of[None, :] < leaf_lengths[:, None]).astype(jnp.float32)[..., None]
    scores = (
        jnp.einsum("lqc,lkc->lqk", query, keys, preferred_element_type=jnp.float32) * score_scale
    )
    scores = jnp.where(visible[None], scores, -jnp.inf)
    top = jnp.max(scores, axis=-1, keepdims=True)
    expo = jnp.exp(scores - top)
    probs = expo / jnp.sum(expo, axis=-1, keepdims=True)
    probs_b = probs.astype(jnp.bfloat16)
    outputs = jnp.einsum("lqk,lkc->lqc", probs_b, values, preferred_element_type=jnp.float32)
    attention = (outputs * live).astype(jnp.bfloat16).reshape(rows, heads, LAT)
    masked_f = grad_out.reshape(leaves, leaf_rows * heads, LAT).astype(jnp.float32) * live
    masked = masked_f.astype(jnp.bfloat16)
    dprobs = jnp.einsum("lqc,lkc->lqk", masked, values, preferred_element_type=jnp.float32)
    delta = jnp.sum(masked_f * outputs, axis=-1)
    dscores = (score_scale * probs * (dprobs - delta[..., None])).astype(jnp.bfloat16)
    grad_keys = jnp.einsum("lqk,lqc->lkc", dscores, query, preferred_element_type=jnp.float32)
    grad_values = jnp.einsum("lqk,lqc->lkc", probs_b, masked, preferred_element_type=jnp.float32)
    grad_keys = jnp.concatenate(
        [grad_keys[:, :, :LAT] + grad_values, grad_keys[:, :, LAT:]], axis=2
    )
    node_terms = grad_keys[:, : 3 * NODE_ROWS].reshape(leaves * 3, NODE_ROWS, width)
    own_terms = grad_keys[:, 3 * NODE_ROWS :].reshape(rows, width)
    head_shares = sum_at_owner(node_terms.astype(jnp.bfloat16), "head", 1)
    owned = node_latent.shape[0]
    spread = jnp.dot(
        picker.T.astype(jnp.float32),
        head_shares.reshape(leaves * 3, -1),
        precision=lax.Precision.HIGHEST,
    )
    arrived = lax.all_to_all(
        spread.astype(jnp.bfloat16), "leaf", split_axis=0, concat_axis=0, tiled=True
    ).astype(spread.dtype)
    mine = jnp.sum(arrived.reshape(-1, owned, arrived.shape[1]), axis=0)
    node_grad = mine.reshape(node_latent.shape).astype(jnp.bfloat16)
    leaf_grad = lax.psum(own_terms, "head").astype(jnp.bfloat16)
    return (attention, node_grad, leaf_grad)


def solution(mesh):
    return jax.shard_map(
        body,
        mesh=mesh,
        in_specs=(
            P("leaf", "head", None),
            P("leaf", None),
            P("leaf", "head", None),
            P("leaf", "head", None),
            P("leaf", None),
            P("leaf"),
        ),
        out_specs=(P("leaf", "head", None), P("leaf", "head", None), P("leaf", None)),
        check_vma=False,
    )
```

profile of v0, /device:TPU:1, one launch (start us, length us, event | category | flops | bytes accessed | tf_op | source)
XLA Modules:
  0.0 187.5 jit_solution(587049199212427704)
XLA Ops:
  0.6 1.9 %broadcast_in_dim.18 = bf16[64,1,12,576]{3,2,1,0:T(8,128)(2,1)} broadcast(bf16[12,576]{1,0:T(8,128)(2,1)} %bitcast.35), dimensions={2,3} | broadcast | bytes 898560 | tf_op jit(solution)/shard_map/broadcast_in_dim | solution.py:16
  2.5 0.0 copy-start.4
  2.5 13.1 %all-to-all-start = ((bf16[64,1,12,576]{3,2,1,0:T(8,128)(2,1)}), bf16[64,1,12,576]{3,2,1,0:T(8,128)(2,1)S(1)}, u32[]{:S(2)}, u32[]{:S(2)}) async-start(bf16[64,1,12,576]{3,2,1,0:T(8,128)(2,1)} %broadcast_in_dim.18), calls=%async_computation | async-start | bytes 2621440 | tf_op jit(solution)/shard_map/all_to_all | solution.py:15
  15.6 0.0 copy-done.4
  15.6 0.1 eq.15
  15.7 32.9 %all-to-all-done = bf16[64,1,12,576]{3,2,1,0:T(8,128)(2,1)S(1)} async-done(((bf16[64,1,12,576]{3,2,1,0:T(8,128)(2,1)}), bf16[64,1,12,576]{3,2,1,0:T(8,128)(2,1)S(1)}, u32[]{:S(2)}, u32[]{:S(2)}) %all-to-all-start) | async-done | bytes 884768 | tf_op jit(solution)/shard_map/all_to_all | solution.py:15
  48.6 0.9 reshape_reshape.6
  49.5 0.3 convolution_convert_fusion.1
  49.8 0.2 broadcast_in_dim.23
  50.0 0.0 copy-start.2
  50.0 1.0 broadcast_in_dim.24
  51.0 0.0 copy-start.1
  51.0 12.5 %all-to-all-start.1 = ((bf16[8,6,12,576]{3,2,1,0:T(8,128)(2,1)}), bf16[8,6,12,576]{3,2,1,0:T(8,128)(2,1)S(1)}, u32[]{:S(2)}, u32[]{:S(2)}) async-start(bf16[8,6,12,576]{3,2,1,0:T(8,128)(2,1)} %broadcast_in_dim.24), calls=%async_computation.1 | async-start | bytes 1966080 | tf_op jit(solution)/shard_map/all_to_all | solution.py:15
  63.5 0.0 copy-done.2
  63.5 0.2 copy.23
  63.6 0.0 copy-start.3
  63.7 0.9 copy.25
  64.5 0.0 copy-done.1
  64.5 2.0 %copy.26 = bf16[128,8,576]{2,1,0:T(8,128)(2,1)} copy(bf16[128,8,576]{0,2,1:T(8,128)(2,1)S(1)} %copy-done.1) | data formatting | bytes 2359296 | tf_op args[0]
  66.6 0.0 copy-done.3
  66.6 0.1 compare_convert_fusion
  66.6 0.9 compare_or_fusion
  67.5 16.5 %all-to-all-done.1 = bf16[8,6,12,576]{3,2,1,0:T(8,128)(2,1)S(1)} async-done(((bf16[8,6,12,576]{3,2,1,0:T(8,128)(2,1)}), bf16[8,6,12,576]{3,2,1,0:T(8,128)(2,1)S(1)}, u32[]{:S(2)}, u32[]{:S(2)}) %all-to-all-start.1) | async-done | bytes 663584 | tf_op jit(solution)/shard_map/all_to_all | solution.py:15
  84.0 0.1 copy.22
  84.1 0.4 reshape_reshape.7
  84.5 0.0 copy-start
  84.5 1.2 copy.24
  85.7 0.3 copy-done
  86.0 2.5 %fusion.9 = f32[2,512,352]{1,2,0:T(8,128)S(1)} fusion(bf16[2,512,576]{2,1,0:T(8,128)(2,1)S(1)} %bitcast.30, bf16[2,64,576]{1,2,0:T(8,128)(2,1)} %copy.25, bf16[2,288,576]{1,2,0:T(8,128)(2,1)} %copy.24, pred[512,352]{0,1:T(8,128)(4,1)} %compare_or_fusion), kind=kOutput, calls=%fused_computation.18 | convolution fusion | flops 417579008 | bytes 3612672 | tf_op jit(solution)/shard_map/lqc,lkc->lqk/dot_general | solution.py:67
  88.5 1.4 fusion.31
  89.9 2.2 %fusion.18 = f32[2,512,512]{2,1,0:T(8,128)S(1)} fusion(bf16[2,64,576]{1,2,0:T(8,128)(2,1)} %copy.25, bf16[2,288,576]{1,2,0:T(8,128)(2,1)} %copy.24, f32[2,512]{1,0:T(2,128)S(1)} %get-tuple-element.12, f32[2,512,352]{1,2,0:T(8,128)S(1)} %fusion.9), kind=kOutput, calls=%fused_computation.31 | convolution fusion | flops 371623264 | bytes 4354048 | tf_op jit(solution)/shard_map/lqk,lkc->lqc/dot_general | solution.py:74
  92.1 3.0 %fusion.4 = (f32[2,512]{1,0:T(2,128)S(1)}, bf16[2,512,512]{2,1,0:T(8,128)(2,1)}, bf16[2,512,512]{2,1,0:T(8,128)(2,1)}) fusion(f32[2,512,512]{2,1,0:T(8,128)S(1)} %fusion.18, f32[2,512]{1,0:T(2,128)S(1)} %compare_convert_fusion, bf16[2,512,512]{2,1,0:T(8,128)(2,1)} %bitcast.32), kind=kLoop, calls=%fused_computation.7 | loop fusion | flops 3668992 | bytes 5251072 | tf_op jit(solution)/shard_map/reduce_sum | solution.py:79
  95.1 5.2 %fusion.11 = f32[2,352,576]{1,2,0:T(8,128)} fusion(bf16[2,512,576]{2,1,0:T(8,128)(2,1)} %bitcast.29, bf16[2,512,512]{2,1,0:T(8,128)(2,1)} %get-tuple-element.11, f32[2,512]{1,0:T(2,128)S(1)} %get-tuple-element.9, f32[2,512,352]{1,2,0:T(8,128)} %get-tuple-element.13, f32[2,512]{1,0:T(2,128)S(1)} %get-tuple-element.12, bf16[2,64,576]{1,2,0:T(8,128)(2,1)} %copy.25, ...), kind=kOutput, calls=%fused_computation.20 | convolution fusion | flops 787578880 | bytes 6111232 | tf_op jit(solution)/shard_map/lqk,lqc->lkc/dot_general | solution.py:81
  100.3 2.5 %slice_add_fusion = f32[2,352,512]{1,2,0:T(8,128)S(1)} fusion(f32[2,352,576]{1,2,0:T(8,128)} %fusion.11, bf16[2,512,512]{2,1,0:T(8,128)(2,1)} %get-tuple-element.11, f32[2,512]{1,0:T(2,128)S(1)} %get-tuple-element.12, f32[2,512,352]{1,2,0:T(8,128)S(1)} %fusion.9), kind=kOutput, calls=%fused_computation.12 | convolution fusion | flops 370541920 | bytes 6819840 | tf_op jit(solution)/shard_map/lqk,lqc->lkc/dot_general | solution.py:82
  102.8 0.9 slice.22
  103.7 0.1 maximum_convert_fusion
  103.9 0.6 copy.32
  104.4 0.2 convert_element_type.66
  104.6 0.1 copy.33
  104.7 35.8 %all_to_all.24 = bf16[8,6,12,576]{3,2,1,0:T(8,128)(2,1)S(1)} all-to-all(bf16[8,6,12,576]{3,2,1,0:T(8,128)(2,1)S(1)} %copy.33), channel_id=1, replica_groups=mesh['leaf'=64,'head'=8] {'head'}, dimensions={0} | all-to-all | bytes 1327104 | tf_op jit(solution)/shard_map/all_to_all | solution.py:38
  140.5 0.2 convert_reduce_fusion
  140.7 0.1 reshape.165
  140.8 1.0 fusion.1
  141.8 0.5 broadcast.139
  142.3 1.3 reduce.2
  143.5 1.2 reshape.168
  144.7 6.0 %all-to-all-start.3 = ((bf16[64,2,3456]{2,1,0:T(2,128)(2,1)}), bf16[64,2,3456]{2,1,0:T(2,128)(2,1)S(1)}, u32[]{:S(2)}, u32[]{:S(2)}) async-start(bf16[64,2,3456]{2,1,0:T(2,128)(2,1)} %reshape.168), calls=%async_computation.3 | async-start | bytes 1769472 | tf_op jit(solution)/shard_map/all_to_all | solution.py:95
  150.7 0.2 pad_maximum_fusion.1
  151.0 0.2 copy.35
  151.2 32.5 %all-reduce.1 = bf16[128,576]{1,0:T(8,128)(2,1)S(1)} all-reduce(f32[128,576]{1,0:T(8,128)S(1)} %bitcast.31), channel_id=1, replica_groups=mesh['leaf'=64,'head'=8] {'head'}, use_global_device_ids=true, to_apply=%region_5.6 | all-reduce | flops 73728 | bytes 442368 | tf_op jit(solution)/shard_map/psum | solution.py:100
  183.7 0.8 copy.36
  184.4 0.0 all-to-all-done.3
  184.4 0.7 reshape.169
  185.2 1.7 reduce_sum.42
  186.8 0.7 convert_element_type.69
  (3 shorter events, 0.0 us)
Async XLA Ops:
  2.5 13.1 %copy-start.4 = (s32[2,3]{1,0:T(2,128)S(1)}, s32[2,3]{1,0:T(2,128)}, u32[]{:S(2)}) copy-start(s32[2,3]{1,0:T(2,128)} %param.10) | copy-start | bytes 76
  2.5 46.1 %all-to-all-start = ((bf16[64,1,12,576]{3,2,1,0:T(8,128)(2,1)}), bf16[64,1,12,576]{3,2,1,0:T(8,128)(2,1)S(1)}, u32[]{:S(2)}, u32[]{:S(2)}) async-start(bf16[64,1,12,576]{3,2,1,0:T(8,128)(2,1)} %broadcast_in_dim.18), calls=%async_computation | async-start | bytes 2621440 | tf_op jit(solution)/shard_map/all_to_all | solution.py:15
  50.0 13.5 %copy-start.2 = (bf16[128,576]{0,1:T(8,128)(2,1)S(1)}, bf16[128,576]{0,1:T(8,128)(2,1)}, u32[]{:S(2)}) copy-start(bf16[128,576]{0,1:T(8,128)(2,1)} %param.7) | copy-start | bytes 442372
  51.0 13.5 %copy-start.1 = (bf16[128,8,576]{0,2,1:T(8,128)(2,1)S(1)}, bf16[128,8,576]{0,2,1:T(8,128)(2,1)}, u32[]{:S(2)}) copy-start(bf16[128,8,576]{0,2,1:T(8,128)(2,1)} %param.6) | copy-start | bytes 3538948
  51.0 33.0 %all-to-all-start.1 = ((bf16[8,6,12,576]{3,2,1,0:T(8,128)(2,1)}), bf16[8,6,12,576]{3,2,1,0:T(8,128)(2,1)S(1)}, u32[]{:S(2)}, u32[]{:S(2)}) async-start(bf16[8,6,12,576]{3,2,1,0:T(8,128)(2,1)} %broadcast_in_dim.24), calls=%async_computation.1 | async-start | bytes 1966080 | tf_op jit(solution)/shard_map/all_to_all | solution.py:15
  63.6 2.9 %copy-start.3 = (s32[2]{0:T(128)S(1)}, s32[2]{0:T(128)}, u32[]{:S(2)}) copy-start(s32[2]{0:T(128)} %param.11) | copy-start | bytes 28
  84.5 1.5 copy-start
  144.7 39.7 %all-to-all-start.3 = ((bf16[64,2,3456]{2,1,0:T(2,128)(2,1)}), bf16[64,2,3456]{2,1,0:T(2,128)(2,1)S(1)}, u32[]{:S(2)}, u32[]{:S(2)}) async-start(bf16[64,2,3456]{2,1,0:T(2,128)(2,1)} %reshape.168), calls=%async_computation.3 | async-start | bytes 1769472 | tf_op jit(solution)/shard_map/all_to_all | solution.py:95
where the time goes:
time: 190 us; the launch traced here: 188 us
  blocking collectives  68.2 us (36%)
  waiting for transfers between devices  49.4 us (26%)
  starting transfers between devices  31.6 us (17%)
  local copies, waits for them, and re-layouts  15.1 us (8%)
  matrix products  13.6 us (7%)
  other arithmetic  8.84 us (5%)
    all_to_all x2, waiting for transfers between devices, from_everyone(): lax.all_to_all(jnp.broadcast_to(shard[None], (devices, *shard.shape)), ax...  49.4 us
    all_to_all x1, blocking collectives, sum_at_owner(): lax.all_to_all(pieces, axis, split_axis=0, concat_axis=0, tiled=True)  35.8 us
    psum x1, blocking collectives, body(): leaf_grad = lax.psum(own_terms, 'head').astype(jnp.bfloat16)  32.5 us
    all_to_all x2, starting transfers between devices, from_everyone(): lax.all_to_all(jnp.broadcast_to(shard[None], (devices, *shard.shape)), ax...  25.6 us
    all_to_all x1, starting transfers between devices, body(): lax.all_to_all(spread.astype(jnp.bfloat16), 'leaf', split_axis=0, concat_...  6.03 us
    dot_general x1, matrix products, body(): jnp.einsum('lqk,lqc->lkc', dscores, query, preferred_element_type=jnp.flo...  5.18 us
    unnamed x15, local copies, waits for them, and re-layouts  5.12 us
  transfers between devices with their start and end apart: 3, of which 2 were waited for; matrix products, arithmetic and copies ran while one was open for 3% of the time, Pallas kernels for 0%

commit v1 on v0

v1 whole, which is shorter than its diff:
```python
import functools

import jax
import jax.numpy as jnp
from jax import lax
from jax.experimental import pallas as pl
from jax.experimental.pallas import tpu as pltpu
from jax.sharding import PartitionSpec as P

MESH = pl.DeviceIdType.MESH
ZLO, XS, YS, ZHI = 2, 4, 8, 4
LAT = 512
LATW = 576
SLICE = 12
UNIT = 32
score_scale = 192.0 ** (-0.5)
F32 = jnp.float32
BF16 = jnp.bfloat16


def place():
    leaf, head = lax.axis_index("leaf"), lax.axis_index("head")
    return leaf // (XS * YS), (leaf // YS) % XS, leaf % YS, head // 2, head % 2


def device(zlo, x, y, zhi, core):
    return ((zlo * XS + x) * YS + y, zhi * 2 + core)


def pack(rows, ref, at):
    for block in range(4):
        part, below = block // 2, block % 2
        ref[part, at + below * SLICE : at + (below + 1) * SLICE, :] = rows[
            :, block * 128 : (block + 1) * 128
        ]
    ref[1, at + 24 : at + 30, :] = jnp.concatenate(
        [rows[0:6, LAT:LATW], rows[6:12, LAT:LATW]], axis=1
    )


def unpack(part, value, ref, at):
    for below in range(2):
        block = part * 2 + below
        ref[at : at + SLICE, block * 128 : (block + 1) * 128] = value[
            below * SLICE : (below + 1) * SLICE, :
        ]
    if part == 1:
        ref[at : at + 6, LAT:LATW] = value[24:30, 0:64]
        ref[at + 6 : at + 12, LAT:LATW] = value[24:30, 64:128]


def kernel(
    q_hbm, g_hbm, lat_hbm, ids_hbm, node_ref, ids_ref, len_ref,
    att_hbm, node_out, own_out,
    qb, gb, kb, kf, dk, pk, pbt, dst, att,
    ids_all,
    col_a, col_b, xs, xr_a, xr_b, zs, zr, zs2, zr2, xs2, xr2, ys, yr,
    os_, or_, ag,
    sem_local, sem_q, sem_att, sem_ids, sem_y, sem_x, sem_z, sem_z2, sem_x2, sem_y2, sem_o, sem_ag, sem_fin,
):
    zlo, x, y, zhi, core = place()
    other = 1 - core
    half = qb.shape[0] // 2
    own_rows = kb.shape[0] - kf.shape[0]
    columns = ZLO * YS
    col, xr = (col_a, col_b), (xr_a, xr_b)

    def remote(src, dst_, sems, index, where):
        return pltpu.make_async_remote_copy(
            src_ref=src, dst_ref=dst_, send_sem=sems.at[(0, *index)], recv_sem=sems.at[(1, *index)],
            device_id=where, device_id_type=MESH,
        )

    def column_peer(k):
        return device(lax.rem(zlo + k // YS, ZLO), x, lax.rem(y + k % YS, YS), zhi, core)

    def x_peer(o, c):
        return device(zlo, lax.rem(x + o, XS), y, zhi, lax.rem(core + c, 2))

    def z_peer(o):
        return device(zlo, x, y, lax.rem(zhi + o, ZHI), core)

    x_moves = [(o, c) for o in range(XS) for c in range(2) if o or c]

    barrier = pltpu.get_barrier_semaphore()

    @pl.loop(1, columns)
    def _(k):
        pl.semaphore_signal(barrier, inc=1, device_id=column_peer(k), device_id_type=MESH)

    for o, c in x_moves:
        pl.semaphore_signal(barrier, inc=1, device_id=x_peer(o, c), device_id_type=MESH)
    for o in range(1, ZHI):
        pl.semaphore_signal(barrier, inc=1, device_id=z_peer(o), device_id_type=MESH)

    locals_in = [
        pltpu.make_async_copy(q_hbm.at[pl.ds(core * half, half)], qb.at[pl.ds(0, half)], sem_local.at[0]),
        pltpu.make_async_copy(g_hbm.at[pl.ds(core * half, half)], gb.at[pl.ds(0, half)], sem_local.at[1]),
        pltpu.make_async_copy(
            lat_hbm.at[pl.ds(core * own_rows, own_rows)], kb.at[pl.ds(kf.shape[0], own_rows)], sem_local.at[2]
        ),
    ]
    for copy in locals_in:
        copy.start()

    mine = zlo * YS + y
    pk[0, :, 0:UNIT, :] = jnp.zeros((2, UNIT, 128), F32)
    pack(node_ref[...].astype(F32), pk.at[0], 0)
    for part in range(2):
        col[part][mine] = pk[0, part, 0:UNIT, :].astype(BF16)
    for leaf in range(2):
        for s in range(3):
            ids_all[0, leaf, s] = ids_ref[leaf, s]

    pl.semaphore_wait(barrier, columns - 1 + len(x_moves) + ZHI - 1)

    def ids_copy(o):
        return remote(ids_hbm, ids_all.at[o], sem_ids, (o,), x_peer(o, 0))

    def y_copy(part, k):
        return remote(col[part].at[mine], col[part].at[mine], sem_y, (part, k), column_peer(k))

    for o in range(1, XS):
        ids_copy(o).start()
    for part in range(2):

        @pl.loop(1, columns)
        def _(k):
            y_copy(part, k).start()

    swap = [
        remote(q_hbm.at[pl.ds(other * half, half)], qb.at[pl.ds(half, half)], sem_q, (0,), x_peer(0, 1)),
        remote(g_hbm.at[pl.ds(other * half, half)], gb.at[pl.ds(half, half)], sem_q, (1,), x_peer(0, 1)),
    ]
    for copy in swap:
        copy.start()

    for o in range(1, XS):
        ids_copy(o).wait()

    def x_copy(part, o, c):
        return remote(xs.at[part, o, c], xr[part].at[o, c], sem_x, (part, o, c), x_peer(o, c))

    def column_of(node):
        return (node // (XS * YS)) * YS + node % YS

    for part in range(2):

        @pl.loop(1, columns)
        def _(k):
            y_copy(part, k).wait_recv()

        for o in range(XS):
            for c in range(2):
                leaf = lax.rem(core + c, 2)
                for s in range(3):
                    node = ids_all[(XS - o) % XS, leaf, s]
                    piece = col[part][column_of(node)]
                    if o or c:
                        xs[part, o, c, s * UNIT : (s + 1) * UNIT, :] = piece
                    else:
                        xr[part][o, c, s * UNIT : (s + 1) * UNIT, :] = piece
        for o, c in x_moves:
            x_copy(part, o, c).start()

    def z_copy(part, o):
        return remote(zs.at[part], zr.at[part, o], sem_z, (part, o), z_peer(o))

    for part in range(2):
        for o, c in x_moves:
            x_copy(part, o, c).wait_recv()
        for s in range(3):
            from_x = (ids_all[0, core, s] // YS) % XS
            o = lax.rem(x - from_x + XS, XS)
            for c in range(2):
                at = (c * 3 + s) * UNIT
                zs[part, at : at + UNIT, :] = xr[part][o, c, s * UNIT : (s + 1) * UNIT, :]
        for o in range(1, ZHI):
            z_copy(part, o).start()

    def keys_from(part, o, block):
        for u in range(6):
            unpack(part, block[u * UNIT : (u + 1) * UNIT, :], kf, (o * 6 + u) * SLICE)

    for part in range(2):
        keys_from(part, 0, zs[part].astype(F32))
    for part in range(2):
        for o in range(1, ZHI):
            z_copy(part, o).wait_recv()
            keys_from(part, o, zr[part, o].astype(F32))
    node_keys = kf.shape[0]
    for copy in locals_in:
        copy.wait()
    for copy in swap:
        copy.wait()
    kb[0:node_keys, :] = kf[...].astype(BF16)

    length = len_ref[core]
    heads = half // own_rows
    step = min(256, half)

    @pl.loop(0, 2 * half // step)
    def _(b):
        at = pl.multiple_of(b * step, step)
        first = lax.rem(b * step, half)
        query = qb[pl.ds(at, step), :]
        keys = kb[...]
        values = keys[:, :LAT]
        scores = lax.dot_general(keys, query, (((1,), (1,)), ((), ())), preferred_element_type=F32) * score_scale
        row = (first + lax.broadcasted_iota(jnp.int32, (own_rows, step), 1)) // heads
        seen = lax.broadcasted_iota(jnp.int32, (own_rows, step), 0) <= row
        scores = jnp.concatenate(
            [scores[:node_keys], jnp.where(seen, scores[node_keys:], -jnp.inf)], axis=0
        )
        top = jnp.max(scores, axis=0, keepdims=True)
        expo = jnp.exp(scores - top)
        probs = expo * (1.0 / jnp.sum(expo, axis=0, keepdims=True))
        probs_b = probs.astype(BF16)
        live = (first + lax.broadcasted_iota(jnp.int32, (step, LAT), 0)) // heads < length
        masked = jnp.where(live, gb[pl.ds(at, step), :].astype(F32), 0.0).astype(BF16)
        gb[pl.ds(at, step), :] = masked
        dprobs = lax.dot_general(values, masked, (((1,), (1,)), ((), ())), preferred_element_type=F32)
        delta = jnp.sum(probs_b.astype(F32) * dprobs, axis=0, keepdims=True)
        pbt[:, pl.ds(at, step)] = probs_b
        dst[:, pl.ds(at, step)] = (score_scale * probs * (dprobs - delta)).astype(BF16)
        outputs = lax.dot_general(probs_b, values, (((0,), (0,)), ((), ())), preferred_element_type=F32)
        att[pl.ds(at, step), :] = jnp.where(live, outputs, 0.0).astype(BF16)

    att_local = pltpu.make_async_copy(att.at[pl.ds(0, half)], att_hbm.at[pl.ds(core * half, half)], sem_local.at[0])
    att_swap = remote(att.at[pl.ds(half, half)], att_hbm.at[pl.ds(core * half, half)], sem_att, (), x_peer(0, 1))
    att_local.start()
    att_swap.start()

    dk[...] = lax.dot_general(dst[...], qb[...], (((1,), (0,)), ((), ())), preferred_element_type=F32)
    dk[:, :LAT] += lax.dot_general(pbt[...], gb[...], (((1,), (0,)), ((), ())), preferred_element_type=F32)

    def z2_copy(part, o):
        return remote(zs2.at[part, o], zr2.at[part, o], sem_z2, (part, o), z_peer(o))

    for o in range(ZHI):
        back = (ZHI - o) % ZHI
        for u in range(6):
            at = (o * 6 + u) * SLICE
            pack(dk[at : at + SLICE, :], pk.at[back], u * UNIT)
        if back:
            for part in range(2):
                zs2[part, back] = pk[back, part].astype(BF16)
                z2_copy(part, back).start()

    quarter = own_rows // ZHI

    def o_copy(o):
        return remote(os_.at[o], or_.at[o], sem_o, (o,), z_peer(o))

    for o in range(1, ZHI):
        at = pl.multiple_of(node_keys + lax.rem(zhi + o, ZHI) * quarter, quarter)
        os_[o] = dk[pl.ds(at, quarter), :].astype(BF16)
        o_copy(o).start()

    def x2_copy(part, o, c):
        return remote(xs2.at[part, c], xr2.at[part, o, c], sem_x2, (part, o, c), x_peer(o, c))

    for part in range(2):
        total = pk[0, part]
        for o in range(1, ZHI):
            z2_copy(part, o).wait_recv()
            total = total + zr2[part, o].astype(F32)
        total = total.astype(BF16)
        for c in range(2):
            block = total[c * 3 * UNIT : (c + 1) * 3 * UNIT, :]
            xs2[part, c] = block
        xr2[part, 0, 0] = xs2[part, 0]
        for o, c in x_moves:
            x2_copy(part, o, c).start()

    def ag_copy(o):
        return remote(ag.at[0], ag.at[o], sem_ag, (o,), z_peer(o))

    at = pl.multiple_of(node_keys + zhi * quarter, quarter)
    total = dk[pl.ds(at, quarter), :]
    for o in range(1, ZHI):
        o_copy(o).wait_recv()
        total = total + or_[o].astype(F32)
    ag[0] = total.astype(BF16)
    for o in range(1, ZHI):
        ag_copy(o).start()

    def y2_copy(part, k):
        to = lax.rem(zlo + k // YS, ZLO) * YS + lax.rem(y + k % YS, YS)
        return remote(ys.at[part, to], yr.at[part, k], sem_y2, (part, k), column_peer(k))

    for part in range(2):
        for o, c in x_moves:
            x2_copy(part, o, c).wait_recv()

        @pl.loop(0, columns)
        def _(t):
            target = ((t // YS) * XS + x) * YS + t % YS
            acc = jnp.zeros((UNIT, 128), F32)
            for o in range(XS):
                for c in range(2):
                    leaf = lax.rem(core + c, 2)
                    for s in range(3):
                        node = ids_all[o, leaf, s]
                        hit = jnp.where(node == target, 1.0, 0.0).astype(F32)
                        acc = acc + hit * xr2[part, o, c, s * UNIT : (s + 1) * UNIT, :].astype(F32)
            ys[part, t] = acc.astype(BF16)

        @pl.loop(1, columns)
        def _(k):
            y2_copy(part, k).start()

    for o in range(1, ZHI):
        ag_copy(o).wait_recv()
    for o in range(ZHI):
        origin = lax.rem(zhi - o + ZHI, ZHI)
        own_out[core, pl.ds(pl.multiple_of(origin * quarter, quarter), quarter), :] = ag[o]
    fin = remote(own_out.at[core], own_out.at[core], sem_fin, (), x_peer(0, 1))
    fin.start()

    for part in range(2):
        total = ys[part, mine].astype(F32)

        for k in range(1, columns):
            y2_copy(part, k).wait_recv()
            total = total + yr[part, k].astype(F32)
        unpack(part, total, dk, 0)
    node_out[...] = dk[0:SLICE, :].astype(BF16)

    for part in range(2):

        @pl.loop(1, columns)
        def _(k):
            y_copy(part, k).wait_send()
            y2_copy(part, k).wait_send()

        for o, c in x_moves:
            x_copy(part, o, c).wait_send()
            x2_copy(part, o, c).wait_send()
        for o in range(1, ZHI):
            z_copy(part, o).wait_send()
            z2_copy(part, o).wait_send()
    for o in range(1, ZHI):
        o_copy(o).wait_send()
        ag_copy(o).wait_send()
    fin.wait()
    att_local.wait()
    att_swap.wait()


def body(queries, leaf_latent, node_latent, grad_out, leaf_nodes, leaf_lengths):
    rows, heads, width = queries.shape
    total = rows * heads
    own_rows = rows // 2
    node_keys = ZHI * 6 * SLICE
    keys = node_keys + own_rows
    columns = ZLO * YS
    vmem = pl.BlockSpec(memory_space=pltpu.VMEM)
    smem = pl.BlockSpec(memory_space=pltpu.SMEM)
    hbm = pl.BlockSpec(memory_space=pl.ANY)
    dma = pltpu.SemaphoreType.DMA
    flops = 2 * total * keys * (3 * LAT + 2 * LATW)
    att, node_grad, own = pl.pallas_call(
        kernel,
        out_shape=(
            jax.ShapeDtypeStruct((total, LAT), BF16),
            jax.ShapeDtypeStruct((SLICE, width), BF16),
            jax.ShapeDtypeStruct((2, own_rows, width), BF16),
        ),
        in_specs=[hbm, hbm, hbm, hbm, vmem, smem, smem],
        out_specs=(hbm, vmem, vmem),
        scratch_shapes=[
            pltpu.VMEM((total, width), BF16),
            pltpu.VMEM((total, LAT), BF16),
            pltpu.VMEM((keys, width), BF16),
            pltpu.VMEM((node_keys, width), F32),
            pltpu.VMEM((keys, width), F32),
            pltpu.VMEM((ZHI, 2, 6 * UNIT, 128), F32),
            pltpu.VMEM((keys, total), BF16),
            pltpu.VMEM((keys, total), BF16),
            pltpu.VMEM((total, LAT), BF16),
            pltpu.SMEM((XS, 2, 3), jnp.int32),
            pltpu.VMEM((columns, UNIT, 128), BF16),
            pltpu.VMEM((columns, UNIT, 128), BF16),
            pltpu.VMEM((2, XS, 2, 3 * UNIT, 128), BF16),
            pltpu.VMEM((XS, 2, 3 * UNIT, 128), BF16),
            pltpu.VMEM((XS, 2, 3 * UNIT, 128), BF16),
            pltpu.VMEM((2, 6 * UNIT, 128), BF16),
            pltpu.VMEM((2, ZHI, 6 * UNIT, 128), BF16),
            pltpu.VMEM((2, ZHI, 6 * UNIT, 128), BF16),
            pltpu.VMEM((2, ZHI, 6 * UNIT, 128), BF16),
            pltpu.VMEM((2, 2, 3 * UNIT, 128), BF16),
            pltpu.VMEM((2, XS, 2, 3 * UNIT, 128), BF16),
            pltpu.VMEM((2, columns, UNIT, 128), BF16),
            pltpu.VMEM((2, columns, UNIT, 128), BF16),
            pltpu.VMEM((ZHI, own_rows // ZHI, width), BF16),
            pltpu.VMEM((ZHI, own_rows // ZHI, width), BF16),
            pltpu.VMEM((ZHI, own_rows // ZHI, width), BF16),
            dma((3,)),
            dma((2, 2)),
            dma((2,)),
            dma((2, XS)),
            dma((2, 2, columns)),
            dma((2, 2, XS, 2)),
            dma((2, 2, ZHI)),
            dma((2, 2, ZHI)),
            dma((2, 2, XS, 2)),
            dma((2, 2, columns)),
            dma((2, ZHI)),
            dma((2, ZHI)),
            dma((2,)),
        ],
        compiler_params=pltpu.CompilerParams(
            collective_id=0, has_side_effects=True, vmem_limit_bytes=48 * 2**20
        ),
        cost_estimate=pl.CostEstimate(
            flops=flops, bytes_accessed=2 * total * (width + 2 * LAT), transcendentals=total * keys
        ),
        name="leaves",
    )(
        queries.reshape(total, width),
        grad_out.reshape(total, LAT),
        leaf_latent,
        leaf_nodes,
        node_latent.reshape(SLICE, width),
        leaf_nodes,
        leaf_lengths,
    )
    return (
        att.reshape(rows, heads, LAT),
        node_grad.reshape(node_latent.shape),
        own.reshape(rows, width),
    )


def solution(mesh):
    return jax.shard_map(
        body,
        mesh=mesh,
        in_specs=(
            P("leaf", "head", None),
            P("leaf", None),
            P("leaf", "head", None),
            P("leaf", "head", None),
            P("leaf", None),
            P("leaf"),
        ),
        out_specs=(P("leaf", "head", None), P("leaf", "head", None), P("leaf", None)),
        check_vma=False,
    )
```

time: 190 us -> 82.8 us (0.44); the launches traced: 188 us -> 82.6 us
  Pallas kernels: 0 us -> 75 us
  blocking collectives: 68.2 us -> 0 us
  waiting for transfers between devices: 49.4 us -> 0 us
  starting transfers between devices: 31.6 us -> 0 us
  matrix products: 13.6 us -> 0 us
  other arithmetic: 8.84 us -> 0 us
  local copies, waits for them, and re-layouts: 15.1 us -> 6.88 us
    pallas_call x0 -> x1, Pallas kernels: none -> 75 us  [body(): pl.pallas_call(kernel, out_shape=(jax.ShapeDtypeStruct((total, LAT), BF16...]
    all_to_all x3 -> x0, waiting for transfers between devices: 49.4 us -> none  [the longest x2 49.4 us: from_everyone(): lax.all_to_all(jnp.broadcast_to(shard[None], (devices, *shard.shape)), ax...]
    all_to_all x1 -> x0, blocking collectives: 35.8 us -> none  [sum_at_owner(): lax.all_to_all(pieces, axis, split_axis=0, concat_axis=0, tiled=True)]
    psum x1 -> x0, blocking collectives: 32.5 us -> none  [body(): leaf_grad = lax.psum(own_terms, 'head').astype(jnp.bfloat16)]
    all_to_all x3 -> x0, starting transfers between devices: 31.6 us -> none  [the longest x2 25.6 us: from_everyone(): lax.all_to_all(jnp.broadcast_to(shard[None], (devices, *shard.shape)), ax...]
    dot_general x6 -> x0, matrix products: 13.6 us -> none  [the longest x1 5.18 us: body(): jnp.einsum('lqk,lqc->lkc', dscores, query, preferred_element_type=jnp.flo...]
    reduce_sum x3 -> x0, other arithmetic: 4.88 us -> none  [the longest x1 3.03 us: body(): delta = jnp.sum(masked_f * outputs, axis=-1)]
    broadcast_in_dim x3 -> x0, local copies, waits for them, and re-layouts: 3.07 us -> none  [from_everyone(): jnp.broadcast_to(shard[None], (devices, *shard.shape))]
  transfers between devices with their start and end apart: 3 -> 0, of which waited for: 2 -> 0; matrix products, arithmetic and copies ran while one was open for 3% -> 0% of each run, Pallas kernels for 0% -> 0%
where the time goes in v1:
time: 82.8 us; the launch traced here: 82.6 us
  Pallas kernels  75 us (91%)
  local copies, waits for them, and re-layouts  6.88 us (8%)
    pallas_call x1, Pallas kernels, body(): pl.pallas_call(kernel, out_shape=(jax.ShapeDtypeStruct((total, LAT), BF16...  75 us
    unnamed x13, local copies, waits for them, and re-layouts  6.88 us

profile of v1, /device:TPU:1, one launch (start us, length us, event | category | flops | bytes accessed | tf_op | source)
XLA Modules:
  0.0 82.6 jit_solution(6133929113577010971)
XLA Ops:
  0.6 1.1 %copy.10.lat_hbm = bf16[128,576]{1,0:T(8,128)(2,1)S(1)} copy(bf16[128,576]{0,1:T(8,128)(2,1)} %param.7) | data formatting | bytes 294912 | tf_op args[1]
  1.7 0.0 copy-start.1
  1.7 0.0 copy-start.2
  1.7 0.0 copy-start.3
  1.7 2.2 %copy.9 = bf16[128,8,576]{2,1,0:T(8,128)(2,1)S(1)} copy(bf16[128,8,576]{0,2,1:T(8,128)(2,1)} %param.6) | data formatting | bytes 2359296 | tf_op args[0]
  4.0 0.0 copy-done.1
  4.0 0.0 copy-done.2
  4.0 0.0 copy-done.3
  4.0 0.0 copy-start
  4.0 1.2 %copy-done = bf16[128,8,512]{2,1,0:T(8,128)(2,1)S(1)} copy-done((bf16[128,8,512]{2,1,0:T(8,128)(2,1)S(1)}, bf16[128,8,512]{2,1,0:T(8,128)(2,1)}, u32[]{:S(2)}) %copy-start) | copy-done | bytes 1048600
  5.2 75.0 %leaves.1 = (bf16[1024,512]{1,0:T(8,128)(2,1)S(1)}, bf16[12,576]{1,0:T(8,128)(2,1)S(1)}, bf16[2,64,576]{2,1,0:T(8,128)(2,1)S(1)}) custom-call(bf16[1024,576]{1,0:T(8,128)(2,1)S(1)} %bitcast.6, bf16[1024,512]{1,0:T(8,128)(2,1)S(1)} %bitcast.10, bf16[128,576]{1,0:T(8,128)(2,1)S(1)} %copy.10.lat_hbm, s32[2,3]{1,0:T(2,128)S(1)} %copy-done.2, ...), custom_call_target="tpu_custom_call" | custom-call | flops 1937768448 | bytes 3276800 | tf_op jit(solution)/shard_map/leaves/pallas_call | solution.py:363
  80.2 0.8 copy.11
  81.0 1.0 %copy.14 = bf16[128,8,512]{2,1,0:T(8,128)(2,1)} copy(bf16[128,8,512]{2,1,0:T(8,128)(2,1)S(1)} %bitcast.7) | data formatting | bytes 2097152
  82.0 0.6 copy.15
Async XLA Ops:
  1.7 2.3 %copy-start.1 = (bf16[1,12,576]{2,1,0:T(8,128)(2,1)S(1)}, bf16[1,12,576]{2,1,0:T(8,128)(2,1)}, u32[]{:S(2)}) copy-start(bf16[1,12,576]{2,1,0:T(8,128)(2,1)} %param.8) | copy-start | bytes 41476
  1.7 2.3 %copy-start.2 = (s32[2,3]{1,0:T(2,128)S(1)}, s32[2,3]{1,0:T(2,128)}, u32[]{:S(2)}) copy-start(s32[2,3]{1,0:T(2,128)} %ids_ref.1) | copy-start | bytes 76
  1.7 2.3 %copy-start.3 = (s32[2]{0:T(128)S(1)}, s32[2]{0:T(128)}, u32[]{:S(2)}) copy-start(s32[2]{0:T(128)} %len_ref.1) | copy-start | bytes 28
  4.0 1.2 %copy-start = (bf16[128,8,512]{2,1,0:T(8,128)(2,1)S(1)}, bf16[128,8,512]{2,1,0:T(8,128)(2,1)}, u32[]{:S(2)}) copy-start(bf16[128,8,512]{2,1,0:T(8,128)(2,1)} %param.9) | copy-start | bytes 3145732

commit v2 on v1

v2 whole, which is shorter than its diff:
```python
import functools

import jax
import jax.numpy as jnp
from jax import lax
from jax.experimental import pallas as pl
from jax.experimental.pallas import tpu as pltpu
from jax.sharding import PartitionSpec as P

MESH = pl.DeviceIdType.MESH
ZLO, XS, YS, ZHI = 2, 4, 8, 4
LAT = 512
LATW = 576
SLICE = 12
HALF = 6
UNIT = 32
score_scale = 192.0 ** (-0.5)
F32 = jnp.float32
BF16 = jnp.bfloat16


def place():
    leaf, head = lax.axis_index("leaf"), lax.axis_index("head")
    return leaf // (XS * YS), (leaf // YS) % XS, leaf % YS, head // 2, head % 2


def device(zlo, x, y, zhi, core):
    return ((zlo * XS + x) * YS + y, zhi * 2 + core)


def pack(rows, ref, at):
    for block in range(4):
        ref[at + block * HALF : at + (block + 1) * HALF, :] = rows[:, block * 128 : (block + 1) * 128]
    ref[at + 24 : at + 27, :] = jnp.concatenate([rows[0:3, LAT:LATW], rows[3:6, LAT:LATW]], axis=1)


def unpack(value, ref, at):
    for block in range(4):
        ref[at : at + HALF, block * 128 : (block + 1) * 128] = value[block * HALF : (block + 1) * HALF, :]
    ref[at : at + 3, LAT:LATW] = value[24:27, 0:64]
    ref[at + 3 : at + 6, LAT:LATW] = value[24:27, 64:128]


def kernel(
    q_hbm, g_hbm, lat_hbm, ids_hbm, node_hbm, ids_ref, len_ref,
    att_hbm, node_out, own_out,
    qt, qf, qs, qb, gb, lt, lf, nd, kb, kf, sc, dp, dk, pk, pbt, dst, att,
    ids_all, pick,
    col_a, col_b, xs, xr_a, xr_b, zs, zr, zs2, zr2, xs2, xr2, ys, yr,
    os_, or_, ag,
    sem_local, sem_q, sem_att, sem_ids, sem_y, sem_x, sem_z, sem_z2, sem_x2, sem_y2, sem_o, sem_ag, sem_fin,
):
    zlo, x, y, zhi, core = place()
    other = 1 - core
    half = qb.shape[0] // 2
    heads = qt.shape[0]
    node_keys = kf.shape[0]
    part_keys = node_keys // 2
    own_rows = kb.shape[0] - node_keys
    columns = ZLO * YS
    col, xr = (col_a, col_b), (xr_a, xr_b)

    def remote(src, dst_, sems, index, where):
        return pltpu.make_async_remote_copy(
            src_ref=src, dst_ref=dst_, send_sem=sems.at[(0, *index)], recv_sem=sems.at[(1, *index)],
            device_id=where, device_id_type=MESH,
        )

    def column_place(k, sign):
        turn = k // ZLO
        along = YS // 2 + ((turn + 1) // 2) * (1 - 2 * (turn % 2))
        across = ZLO - 1 - k % ZLO
        return (zlo + sign * across + ZLO) % ZLO, (y + sign * along + YS) % YS

    def column_peer(k):
        a, b = column_place(k, 1)
        return device(a, x, b, zhi, core)

    def x_peer(o, c):
        return device(zlo, lax.rem(x + o, XS), y, zhi, lax.rem(core + c, 2))

    def z_peer(o):
        return device(zlo, x, y, lax.rem(zhi + o, ZHI), core)

    x_moves = [(o, c) for o in range(XS) for c in range(2) if o or c]
    node_in = pltpu.make_async_copy(node_hbm, nd, sem_local.at[0])
    node_in.start()

    barrier = pltpu.get_barrier_semaphore()

    @pl.loop(0, columns - 1)
    def _(k):
        pl.semaphore_signal(barrier, inc=1, device_id=column_peer(k), device_id_type=MESH)

    for o, c in x_moves:
        pl.semaphore_signal(barrier, inc=1, device_id=x_peer(o, c), device_id_type=MESH)
    for o in range(1, ZHI):
        pl.semaphore_signal(barrier, inc=1, device_id=z_peer(o), device_id_type=MESH)

    q_in = pltpu.make_async_copy(q_hbm, qt, sem_local.at[1])
    g_in = pltpu.make_async_copy(g_hbm.at[pl.ds(core * half, half)], gb.at[pl.ds(0, half)], sem_local.at[2])
    lat_in = pltpu.make_async_copy(lat_hbm, lt, sem_local.at[3])
    q_in.start()
    g_in.start()
    lat_in.start()

    mine = zlo * YS + y
    for leaf in range(2):
        for s in range(3):
            ids_all[0, leaf, s] = ids_ref[leaf, s]
    pk[0, :, 0:UNIT, :] = jnp.zeros((2, UNIT, 128), F32)
    node_in.wait()
    slice_rows = nd[...].astype(F32)
    for part in range(2):
        pack(slice_rows[part * HALF : (part + 1) * HALF, :], pk.at[0, part], 0)
        col[part][mine] = pk[0, part, 0:UNIT, :].astype(BF16)

    pl.semaphore_wait(barrier, columns - 1 + len(x_moves) + ZHI - 1)

    def ids_copy(o):
        return remote(ids_hbm, ids_all.at[o], sem_ids, (o,), x_peer(o, 0))

    def y_copy(part, k):
        return remote(col[part].at[mine], col[part].at[mine], sem_y, (part, k), column_peer(k))

    for part in range(2):

        @pl.loop(0, columns - 1)
        def _(k):
            y_copy(part, k).start()

        if part == 0:
            for o in range(1, XS):
                ids_copy(o).start()

    g_swap = remote(g_hbm.at[pl.ds(other * half, half)], gb.at[pl.ds(half, half)], sem_q, (1,), x_peer(0, 1))
    g_swap.start()

    q_in.wait()

    @pl.loop(0, heads)
    def _(h):
        for block in range(5):
            piece = qt[h, block * 128 : min((block + 1) * 128, LATW), :].astype(F32)
            if block == 4:
                piece = jnp.concatenate([piece, jnp.zeros((64, piece.shape[1]), F32)], axis=0)
            qf[block, pl.ds(h, 2 * own_rows, stride=heads), :] = jnp.transpose(piece)

    for block in range(5):
        to = slice(block * 128, min((block + 1) * 128, LATW))
        for leaf_of, rows_to in ((core, qb), (other, qs)):
            piece = qf[block, pl.ds(pl.multiple_of(leaf_of * half, half), half), :].astype(BF16)
            rows_to[0:half, to] = piece[:, : to.stop - to.start]
    q_swap = remote(qs, qb.at[pl.ds(half, half)], sem_q, (0,), x_peer(0, 1))
    q_swap.start()

    for o in range(1, XS):
        ids_copy(o).wait()

    def x_copy(part, o, c):
        return remote(xs.at[part, o, c], xr[part].at[o, c], sem_x, (part, o, c), x_peer(o, c))

    def column_of(node):
        return (node // (XS * YS)) * YS + node % YS

    for part in range(2):

        @pl.loop(0, columns - 1)
        def _(k):
            y_copy(part, k).wait_recv()

        for o in reversed(range(XS)):
            for c in range(2):
                leaf = lax.rem(core + c, 2)
                for s in range(3):
                    node = ids_all[(XS - o) % XS, leaf, s]
                    piece = col[part][column_of(node)]
                    if o or c:
                        xs[part, o, c, s * UNIT : (s + 1) * UNIT, :] = piece
                    else:
                        xr[part][o, c, s * UNIT : (s + 1) * UNIT, :] = piece
                if o or c:
                    x_copy(part, o, c).start()

    lat_in.wait()
    lf[...] = jnp.transpose(lt[...].astype(F32))
    kb[node_keys:, :] = lf[pl.ds(pl.multiple_of(core * own_rows, own_rows), own_rows), :].astype(BF16)

    def z_copy(part, o):
        return remote(zs.at[part], zr.at[part, o], sem_z, (part, o), z_peer(o))

    for part in range(2):
        for o, c in x_moves:
            x_copy(part, o, c).wait_recv()
        for s in range(3):
            from_x = (ids_all[0, core, s] // YS) % XS
            o = lax.rem(x - from_x + XS, XS)
            for c in range(2):
                at = (c * 3 + s) * UNIT
                zs[part, at : at + UNIT, :] = xr[part][o, c, s * UNIT : (s + 1) * UNIT, :]
        for o in (2, 1, 3):
            if o < ZHI:
                z_copy(part, o).start()

    def unpack_keys(part, o, block):
        for u in range(6):
            unpack(block[u * UNIT : (u + 1) * UNIT, :], kf, part * part_keys + (o * 6 + u) * HALF)

    def products(at, count):
        keys = kb[at : at + count, :]
        sc[at : at + count, :] = score_scale * lax.dot_general(
            keys, qb[...], (((1,), (1,)), ((), ())), preferred_element_type=F32
        )
        dp[at : at + count, :] = lax.dot_general(
            keys[:, :LAT], gb[...], (((1,), (1,)), ((), ())), preferred_element_type=F32
        )

    length = len_ref[core]
    g_in.wait()
    g_swap.wait()
    q_swap.wait()
    step = min(256, half)

    def live_rows(at):
        first = lax.rem(at, half)
        return (first + lax.broadcasted_iota(jnp.int32, (step, LAT), 0)) // heads < length

    @pl.loop(0, 2 * half // step)
    def _(b):
        at = pl.multiple_of(b * step, step)
        gb[pl.ds(at, step), :] = jnp.where(live_rows(at), gb[pl.ds(at, step), :].astype(F32), 0.0).astype(BF16)

    products(node_keys, own_rows)
    for part in range(2):
        unpack_keys(part, 0, zs[part].astype(F32))
    pk[...] = jnp.zeros(pk.shape, F32)
    for part in range(2):
        for o in (1, 3, 2):
            if o < ZHI:
                z_copy(part, o).wait_recv()
                unpack_keys(part, o, zr[part, o].astype(F32))
        at = part * part_keys
        kb[at : at + part_keys, :] = kf[at : at + part_keys, :].astype(BF16)
        products(at, part_keys)

    @pl.loop(0, 2 * half // step)
    def _(b):
        at = pl.multiple_of(b * step, step)
        first = lax.rem(b * step, half)
        row = (first + lax.broadcasted_iota(jnp.int32, (own_rows, step), 1)) // heads
        seen = lax.broadcasted_iota(jnp.int32, (own_rows, step), 0) <= row
        scores = jnp.concatenate(
            [sc[0:node_keys, pl.ds(at, step)], jnp.where(seen, sc[node_keys:, pl.ds(at, step)], -jnp.inf)], axis=0
        )
        dprobs = dp[:, pl.ds(at, step)]
        top = jnp.max(scores, axis=0, keepdims=True)
        expo = jnp.exp(scores - top)
        probs = expo * (1.0 / jnp.sum(expo, axis=0, keepdims=True))
        probs_b = probs.astype(BF16)
        delta = jnp.sum(probs_b.astype(F32) * dprobs, axis=0, keepdims=True)
        pbt[:, pl.ds(at, step)] = probs_b
        dst[:, pl.ds(at, step)] = (score_scale * probs * (dprobs - delta)).astype(BF16)

    def z2_copy(part, o):
        return remote(zs2.at[part, o], zr2.at[part, o], sem_z2, (part, o), z_peer(o))

    def key_terms(at, count):
        dk[at : at + count, :] = lax.dot_general(
            dst[at : at + count, :], qb[...], (((1,), (0,)), ((), ())), preferred_element_type=F32
        )
        dk[at : at + count, :LAT] += lax.dot_general(
            pbt[at : at + count, :], gb[...], (((1,), (0,)), ((), ())), preferred_element_type=F32
        )

    for part in range(2):
        key_terms(part * part_keys, part_keys)
        for o in (2, 1, 3, 0):
            if o < ZHI:
                back = (ZHI - o) % ZHI
                for u in range(6):
                    at = part * part_keys + (o * 6 + u) * HALF
                    pack(dk[at : at + HALF, :], pk.at[back, part], u * UNIT)
                if back:
                    zs2[part, back] = pk[back, part].astype(BF16)
                    z2_copy(part, back).start()
    key_terms(node_keys, own_rows)

    quarter = own_rows // ZHI

    def o_copy(o):
        return remote(os_.at[o], or_.at[o], sem_o, (o,), z_peer(o))

    for o in range(1, ZHI):
        at = pl.multiple_of(node_keys + lax.rem(zhi + o, ZHI) * quarter, quarter)
        os_[o] = dk[pl.ds(at, quarter), :].astype(BF16)
        o_copy(o).start()

    for group in range(pick.shape[1] // 128):
        lane = lax.broadcasted_iota(jnp.int32, pick.shape[:1] + (128,), 1)
        line = lax.broadcasted_iota(jnp.int32, pick.shape[:1] + (128,), 0)
        goal = jnp.full(lane.shape, -1, jnp.int32)
        for quad in range(4):
            term = group * 4 + quad
            o, c, s = term // 6, (term // 3) % 2, term % 3
            node = ids_all[o, lax.rem(core + c, 2), s]
            place_ = jnp.where((node // YS) % XS == x, column_of(node), -1)
            goal = jnp.where(lane // UNIT == quad, place_, goal)
        hit = (line // UNIT == goal) & (line % UNIT == lane % UNIT)
        pick[:, group * 128 : (group + 1) * 128] = jnp.where(hit, 1.0, 0.0).astype(BF16)

    @pl.loop(0, 2 * half // step)
    def _(b):
        at = pl.multiple_of(b * step, step)
        outputs = lax.dot_general(
            pbt[:, pl.ds(at, step)], kb[:, :LAT], (((0,), (0,)), ((), ())), preferred_element_type=F32
        )
        att[pl.ds(at, step), :] = jnp.where(live_rows(at), outputs, 0.0).astype(BF16)

    att_local = pltpu.make_async_copy(att.at[pl.ds(0, half)], att_hbm.at[pl.ds(core * half, half)], sem_local.at[4])
    att_swap = remote(att.at[pl.ds(half, half)], att_hbm.at[pl.ds(core * half, half)], sem_att, (), x_peer(0, 1))
    att_local.start()
    att_swap.start()

    def x2_copy(part, o, c):
        return remote(xs2.at[part, c], xr2.at[part, o, c], sem_x2, (part, o, c), x_peer(o, c))

    for part in range(2):
        total = pk[0, part]
        for o in range(1, ZHI):
            z2_copy(part, o).wait_recv()
            total = total + zr2[part, o].astype(F32)
        total = total.astype(BF16)
        for c in range(2):
            xs2[part, c] = total[c * 3 * UNIT : (c + 1) * 3 * UNIT, :]
        xr2[part, 0, 0] = total[0 : 3 * UNIT, :]
        for o, c in reversed(x_moves):
            x2_copy(part, o, c).start()

    def ag_copy(o):
        return remote(ag.at[0], ag.at[o], sem_ag, (o,), z_peer(o))

    at = pl.multiple_of(node_keys + zhi * quarter, quarter)
    total = dk[pl.ds(at, quarter), :]
    for o in range(1, ZHI):
        o_copy(o).wait_recv()
        total = total + or_[o].astype(F32)
    ag[0] = total.astype(BF16)
    for o in range(1, ZHI):
        ag_copy(o).start()

    def y2_copy(part, k):
        a, b = column_place(k, 1)
        return remote(ys.at[part, a * YS + b], yr.at[part, k], sem_y2, (part, k), column_peer(k))

    for part in range(2):
        for o, c in x_moves:
            x2_copy(part, o, c).wait_recv()
        terms = xr2[part].reshape(XS * 2 * 3 * UNIT, 128)
        sums = jnp.dot(pick[...], terms, preferred_element_type=F32)
        ys[part] = sums.astype(BF16).reshape(columns, UNIT, 128)

        @pl.loop(0, columns - 1)
        def _(k):
            y2_copy(part, k).start()

    for o in range(1, ZHI):
        ag_copy(o).wait_recv()
    for o in range(ZHI):
        origin = lax.rem(zhi - o + ZHI, ZHI)
        own_out[core, pl.ds(pl.multiple_of(origin * quarter, quarter), quarter), :] = ag[o]
    fin = remote(own_out.at[core], own_out.at[core], sem_fin, (), x_peer(0, 1))
    fin.start()

    for part in range(2):

        @pl.loop(0, columns - 1)
        def _(k):
            y_copy(part, k).wait_send()

        for o, c in x_moves:
            x_copy(part, o, c).wait_send()
            x2_copy(part, o, c).wait_send()
        for o in range(1, ZHI):
            z_copy(part, o).wait_send()
            z2_copy(part, o).wait_send()
    for o in range(1, ZHI):
        o_copy(o).wait_send()
        ag_copy(o).wait_send()
    att_local.wait()
    att_swap.wait()

    for part in range(2):
        for k in range(columns - 1):
            y2_copy(part, k).wait_recv()
        total = ys[part, mine].astype(F32)
        for k in range(columns - 1):
            total = total + yr[part, k].astype(F32)
        unpack(total, dk, part * HALF)
    node_out[...] = dk[0:SLICE, :].astype(BF16)
    fin.wait()
    for part in range(2):

        @pl.loop(0, columns - 1)
        def _(k):
            y2_copy(part, k).wait_send()


def body(queries, leaf_latent, node_latent, grad_out, leaf_nodes, leaf_lengths):
    rows, heads, width = queries.shape
    total = rows * heads
    own_rows = rows // 2
    node_keys = ZHI * 6 * SLICE
    keys = node_keys + own_rows
    columns = ZLO * YS
    vmem = pl.BlockSpec(memory_space=pltpu.VMEM)
    smem = pl.BlockSpec(memory_space=pltpu.SMEM)
    hbm = pl.BlockSpec(memory_space=pl.ANY)
    dma = pltpu.SemaphoreType.DMA
    flops = 2 * total * keys * (3 * LAT + 2 * LATW)
    att, node_grad, own = pl.pallas_call(
        kernel,
        out_shape=(
            pltpu.VMEM((total, LAT), BF16),
            pltpu.VMEM((SLICE, width), BF16),
            pltpu.VMEM((2, own_rows, width), BF16),
        ),
        in_specs=[hbm, hbm, hbm, hbm, hbm, smem, smem],
        out_specs=(hbm, vmem, vmem),
        scratch_shapes=[
            pltpu.VMEM((heads, width, rows), BF16),
            pltpu.VMEM((5, total, 128), F32),
            pltpu.VMEM((total // 2, width), BF16),
            pltpu.VMEM((total, width), BF16),
            pltpu.VMEM((total, LAT), BF16),
            pltpu.VMEM((width, rows), BF16),
            pltpu.VMEM((rows, width), F32),
            pltpu.VMEM((SLICE, width), BF16),
            pltpu.VMEM((keys, width), BF16),
            pltpu.VMEM((node_keys, width), F32),
            pltpu.VMEM((keys, total), F32),
            pltpu.VMEM((keys, total), F32),
            pltpu.VMEM((keys, width), F32),
            pltpu.VMEM((ZHI, 2, 6 * UNIT, 128), F32),
            pltpu.VMEM((keys, total), BF16),
            pltpu.VMEM((keys, total), BF16),
            pltpu.VMEM((total, LAT), BF16),
            pltpu.SMEM((XS, 2, 3), jnp.int32),
            pltpu.VMEM((columns * UNIT, XS * 6 * UNIT), BF16),
            pltpu.VMEM((columns, UNIT, 128), BF16),
            pltpu.VMEM((columns, UNIT, 128), BF16),
            pltpu.VMEM((2, XS, 2, 3 * UNIT, 128), BF16),
            pltpu.VMEM((XS, 2, 3 * UNIT, 128), BF16),
            pltpu.VMEM((XS, 2, 3 * UNIT, 128), BF16),
            pltpu.VMEM((2, 6 * UNIT, 128), BF16),
            pltpu.VMEM((2, ZHI, 6 * UNIT, 128), BF16),
            pltpu.VMEM((2, ZHI, 6 * UNIT, 128), BF16),
            pltpu.VMEM((2, ZHI, 6 * UNIT, 128), BF16),
            pltpu.VMEM((2, 2, 3 * UNIT, 128), BF16),
            pltpu.VMEM((2, XS, 2, 3 * UNIT, 128), BF16),
            pltpu.VMEM((2, columns, UNIT, 128), BF16),
            pltpu.VMEM((2, columns, UNIT, 128), BF16),
            pltpu.VMEM((ZHI, own_rows // ZHI, width), BF16),
            pltpu.VMEM((ZHI, own_rows // ZHI, width), BF16),
            pltpu.VMEM((ZHI, own_rows // ZHI, width), BF16),
            dma((5,)),
            dma((2, 2)),
            dma((2,)),
            dma((2, XS)),
            dma((2, 2, columns)),
            dma((2, 2, XS, 2)),
            dma((2, 2, ZHI)),
            dma((2, 2, ZHI)),
            dma((2, 2, XS, 2)),
            dma((2, 2, columns)),
            dma((2, ZHI)),
            dma((2, ZHI)),
            dma((2,)),
        ],
        compiler_params=pltpu.CompilerParams(
            collective_id=0, has_side_effects=True, vmem_limit_bytes=61 * 2**20
        ),
        cost_estimate=pl.CostEstimate(
            flops=flops, bytes_accessed=2 * total * (width + 2 * LAT), transcendentals=total * keys
        ),
        name="leaves",
    )(
        queries.transpose(1, 2, 0),
        grad_out.reshape(total, LAT),
        leaf_latent.T,
        leaf_nodes,
        node_latent.reshape(SLICE, width),
        leaf_nodes,
        leaf_lengths,
    )
    return (
        att.reshape(rows, heads, LAT),
        node_grad.reshape(node_latent.shape),
        own.reshape(rows, width),
    )


def solution(mesh):
    return jax.shard_map(
        body,
        mesh=mesh,
        in_specs=(
            P("leaf", "head", None),
            P("leaf", None),
            P("leaf", "head", None),
            P("leaf", "head", None),
            P("leaf", None),
            P("leaf"),
        ),
        out_specs=(P("leaf", "head", None), P("leaf", "head", None), P("leaf", None)),
        check_vma=False,
    )
```

time: 82.8 us -> 70 us (0.85)
  Pallas kernels: 75 us -> 66.8 us
  local copies, waits for them, and re-layouts: 6.88 us -> 2.37 us
    pallas_call x1, Pallas kernels: 75 us -> 66.8 us  [body(): pl.pallas_call(kernel, out_shape=(pltpu.VMEM((total, LAT), BF16), pltpu.V...]
    unnamed x13 -> x3, local copies, waits for them, and re-layouts: 6.88 us -> 2.37 us
where the time goes in v2:
time: 70 us; the launch traced here: 69.8 us
  Pallas kernels  66.8 us (95%)
  local copies, waits for them, and re-layouts  2.37 us (3%)
    pallas_call x1, Pallas kernels, body(): pl.pallas_call(kernel, out_shape=(pltpu.VMEM((total, LAT), BF16), pltpu.V...  66.8 us
    unnamed x3, local copies, waits for them, and re-layouts  2.37 us

profile of v2, /device:TPU:1, one launch (start us, length us, event | category | flops | bytes accessed | tf_op | source)
XLA Modules:
  0.0 69.8 jit_solution(8941821895485185437)
XLA Ops:
  0.6 66.8 %leaves.1 = (bf16[1024,512]{1,0:T(8,128)(2,1)S(1)}, bf16[12,576]{1,0:T(8,128)(2,1)S(1)}, bf16[2,64,576]{2,1,0:T(8,128)(2,1)S(1)}) custom-call(bf16[8,576,128]{2,1,0:T(8,128)(2,1)} %bitcast.10, bf16[1024,512]{1,0:T(8,128)(2,1)} %bitcast.11, bf16[576,128]{1,0:T(8,128)(2,1)} %bitcast.12, s32[2,3]{1,0:T(2,128)} %ids_ref.1, bf16[12,576]{1,0:T(8,128)(2,1)} %bitcast.13, ...), custom_call_target="tpu_custom_call" | custom-call | flops 1937768448 | bytes 3276800 | tf_op jit(solution)/shard_map/leaves/pallas_call | solution.py:420
  67.4 1.0 %copy.12 = bf16[128,8,512]{2,1,0:T(8,128)(2,1)} copy(bf16[128,8,512]{2,1,0:T(8,128)(2,1)S(1)} %bitcast.7) | data formatting | bytes 2097152
  68.4 0.6 copy.13
  69.0 0.8 %copy.9 = bf16[128,576]{0,1:T(8,128)(2,1)} copy(bf16[128,576]{1,0:T(8,128)(2,1)S(1)} %bitcast.9) | data formatting | bytes 294912

commit v3 on v2

--- a/solution.py
+++ b/solution.py
@@ -12,8 +12,9 @@
 LAT = 512
 LATW = 576
 SLICE = 12
-HALF = 6
-UNIT = 32
+PARTS = 4
+ROWS = SLICE // PARTS
+UNIT = 16
 score_scale = 192.0 ** (-0.5)
 F32 = jnp.float32
 BF16 = jnp.bfloat16
@@ -21,7 +22,9 @@
 
 def place():
     leaf, head = lax.axis_index("leaf"), lax.axis_index("head")
-    return leaf // (XS * YS), (leaf // YS) % XS, leaf % YS, head // 2, head % 2
+    return (
+        lax.div(leaf, XS * YS), lax.rem(lax.div(leaf, YS), XS), lax.rem(leaf, YS), lax.div(head, 2), lax.rem(head, 2)
+    )
 
 
 def device(zlo, x, y, zhi, core):
@@ -30,23 +33,25 @@
 
 def pack(rows, ref, at):
     for block in range(4):
-        ref[at + block * HALF : at + (block + 1) * HALF, :] = rows[:, block * 128 : (block + 1) * 128]
-    ref[at + 24 : at + 27, :] = jnp.concatenate([rows[0:3, LAT:LATW], rows[3:6, LAT:LATW]], axis=1)
+        ref[at + block * ROWS : at + (block + 1) * ROWS, :] = rows[:, block * 128 : (block + 1) * 128]
+    ref[at + 12 : at + 13, :] = jnp.concatenate([rows[0:1, LAT:LATW], rows[1:2, LAT:LATW]], axis=1)
+    ref[at + 13 : at + 14, 0:64] = rows[2:3, LAT:LATW]
 
 
 def unpack(value, ref, at):
     for block in range(4):
-        ref[at : at + HALF, block * 128 : (block + 1) * 128] = value[block * HALF : (block + 1) * HALF, :]
-    ref[at : at + 3, LAT:LATW] = value[24:27, 0:64]
-    ref[at + 3 : at + 6, LAT:LATW] = value[24:27, 64:128]
+        ref[at : at + ROWS, block * 128 : (block + 1) * 128] = value[block * ROWS : (block + 1) * ROWS, :]
+    ref[at : at + 1, LAT:LATW] = value[12:13, 0:64]
+    ref[at + 1 : at + 2, LAT:LATW] = value[12:13, 64:128]
+    ref[at + 2 : at + 3, LAT:LATW] = value[13:14, 0:64]
 
 
 def kernel(
-    q_hbm, g_hbm, lat_hbm, ids_hbm, node_hbm, ids_ref, len_ref,
+    q_hbm, g_hbm, lat_hbm, ids_hbm, node_hbm, len_hbm,
     att_hbm, node_out, own_out,
     qt, qf, qs, qb, gb, lt, lf, nd, kb, kf, sc, dp, dk, pk, pbt, dst, att,
-    ids_all, pick,
-    col_a, col_b, xs, xr_a, xr_b, zs, zr, zs2, zr2, xs2, xr2, ys, yr,
+    ids_all, want, len_ref, pick,
+    col, xs, xr, zs, zr, zs2, zr2, xs2, xr2, ys, yr,
     os_, or_, ag,
     sem_local, sem_q, sem_att, sem_ids, sem_y, sem_x, sem_z, sem_z2, sem_x2, sem_y2, sem_o, sem_ag, sem_fin,
 ):
@@ -55,10 +60,9 @@
     half = qb.shape[0] // 2
     heads = qt.shape[0]
     node_keys = kf.shape[0]
-    part_keys = node_keys // 2
+    part_keys = node_keys // PARTS
     own_rows = kb.shape[0] - node_keys
     columns = ZLO * YS
-    col, xr = (col_a, col_b), (xr_a, xr_b)
 
     def remote(src, dst_, sems, index, where):
         return pltpu.make_async_remote_copy(
@@ -70,7 +74,7 @@
         turn = k // ZLO
         along = YS // 2 + ((turn + 1) // 2) * (1 - 2 * (turn % 2))
         across = ZLO - 1 - k % ZLO
-        return (zlo + sign * across + ZLO) % ZLO, (y + sign * along + YS) % YS
+        return lax.rem(zlo + sign * across + ZLO, ZLO), lax.rem(y + sign * along + YS, YS)
 
     def column_peer(k):
         a, b = column_place(k, 1)
@@ -87,9 +91,7 @@
     node_in.start()
 
     barrier = pltpu.get_barrier_semaphore()
-
-    @pl.loop(0, columns - 1)
-    def _(k):
+    for k in range(columns - 1):
         pl.semaphore_signal(barrier, inc=1, device_id=column_peer(k), device_id_type=MESH)
 
     for o, c in x_moves:
@@ -104,15 +106,16 @@
     g_in.start()
     lat_in.start()
 
+    ids_in = pltpu.make_async_copy(ids_hbm, ids_all.at[0], sem_local.at[5])
+    len_in = pltpu.make_async_copy(len_hbm, len_ref, sem_local.at[6])
+    ids_in.start()
+    len_in.start()
     mine = zlo * YS + y
-    for leaf in range(2):
-        for s in range(3):
-            ids_all[0, leaf, s] = ids_ref[leaf, s]
-    pk[0, :, 0:UNIT, :] = jnp.zeros((2, UNIT, 128), F32)
+    pk[0, :, 0:UNIT, :] = jnp.zeros((PARTS, UNIT, 128), F32)
     node_in.wait()
     slice_rows = nd[...].astype(F32)
-    for part in range(2):
-        pack(slice_rows[part * HALF : (part + 1) * HALF, :], pk.at[0, part], 0)
+    for part in range(PARTS):
+        pack(slice_rows[part * ROWS : (part + 1) * ROWS, :], pk.at[0, part], 0)
         col[part][mine] = pk[0, part, 0:UNIT, :].astype(BF16)
 
     pl.semaphore_wait(barrier, columns - 1 + len(x_moves) + ZHI - 1)
@@ -123,10 +126,8 @@
     def y_copy(part, k):
         return remote(col[part].at[mine], col[part].at[mine], sem_y, (part, k), column_peer(k))
 
-    for part in range(2):
-
-        @pl.loop(0, columns - 1)
-        def _(k):
+    for part in range(PARTS):
+        for k in range(columns - 1):
             y_copy(part, k).start()
 
         if part == 0:
@@ -136,16 +137,50 @@
     g_swap = remote(g_hbm.at[pl.ds(other * half, half)], gb.at[pl.ds(half, half)], sem_q, (1,), x_peer(0, 1))
     g_swap.start()
 
+    def turn_queries(low, high):
+        @pl.loop(low, high)
+        def _(h):
+            for block in range(5):
+                piece = qt[h, block * 128 : min((block + 1) * 128, LATW), :].astype(F32)
+                if block == 4:
+                    piece = jnp.concatenate([piece, jnp.zeros((64, piece.shape[1]), F32)], axis=0)
+                qf[block, pl.ds(h, 2 * own_rows, stride=heads), :] = jnp.transpose(piece)
+
     q_in.wait()
-
-    @pl.loop(0, heads)
-    def _(h):
-        for block in range(5):
-            piece = qt[h, block * 128 : min((block + 1) * 128, LATW), :].astype(F32)
-            if block == 4:
-                piece = jnp.concatenate([piece, jnp.zeros((64, piece.shape[1]), F32)], axis=0)
-            qf[block, pl.ds(h, 2 * own_rows, stride=heads), :] = jnp.transpose(piece)
-
+    turn_queries(0, heads // 2)
+
+    def column_of(node):
+        return lax.div(node, XS * YS) * YS + lax.rem(node, YS)
+
+    ids_in.wait()
+    len_in.wait()
+    for o in range(1, XS):
+        ids_copy(o).wait()
+    for o in range(XS):
+        for leaf in range(2):
+            for s in range(3):
+                want[o, leaf, s] = column_of(ids_all[o, leaf, s])
+
+    def x_copy(part, o, c):
+        return remote(xs.at[part, o, c], xr[part].at[o, c], sem_x, (part, o, c), x_peer(o, c))
+
+    for part in range(PARTS):
+        for k in range(columns - 1):
+            y_copy(part, k).wait_recv()
+
+        for o in reversed(range(XS)):
+            for c in range(2):
+                leaf = lax.rem(core + c, 2)
+                for s in range(3):
+                    piece = col[part][want[(XS - o) % XS, leaf, s]]
+                    if o or c:
+                        xs[part, o, c, s * UNIT : (s + 1) * UNIT, :] = piece
+                    else:
+                        xr[part][o, c, s * UNIT : (s + 1) * UNIT, :] = piece
+                if o or c:
+                    x_copy(part, o, c).start()
+
+    turn_queries(heads // 2, heads)
     for block in range(5):
         to = slice(block * 128, min((block + 1) * 128, LATW))
         for leaf_of, rows_to in ((core, qb), (other, qs)):
@@ -154,34 +189,6 @@
     q_swap = remote(qs, qb.at[pl.ds(half, half)], sem_q, (0,), x_peer(0, 1))
     q_swap.start()
 
-    for o in range(1, XS):
-        ids_copy(o).wait()
-
-    def x_copy(part, o, c):
-        return remote(xs.at[part, o, c], xr[part].at[o, c], sem_x, (part, o, c), x_peer(o, c))
-
-    def column_of(node):
-        return (node // (XS * YS)) * YS + node % YS
-
-    for part in range(2):
-
-        @pl.loop(0, columns - 1)
-        def _(k):
-            y_copy(part, k).wait_recv()
-
-        for o in reversed(range(XS)):
-            for c in range(2):
-                leaf = lax.rem(core + c, 2)
-                for s in range(3):
-                    node = ids_all[(XS - o) % XS, leaf, s]
-                    piece = col[part][column_of(node)]
-                    if o or c:
-                        xs[part, o, c, s * UNIT : (s + 1) * UNIT, :] = piece
-                    else:
-                        xr[part][o, c, s * UNIT : (s + 1) * UNIT, :] = piece
-                if o or c:
-                    x_copy(part, o, c).start()
-
     lat_in.wait()
     lf[...] = jnp.transpose(lt[...].astype(F32))
     kb[node_keys:, :] = lf[pl.ds(pl.multiple_of(core * own_rows, own_rows), own_rows), :].astype(BF16)
@@ -189,11 +196,11 @@
     def z_copy(part, o):
         return remote(zs.at[part], zr.at[part, o], sem_z, (part, o), z_peer(o))
 
-    for part in range(2):
+    for part in range(PARTS):
         for o, c in x_moves:
             x_copy(part, o, c).wait_recv()
         for s in range(3):
-            from_x = (ids_all[0, core, s] // YS) % XS
+            from_x = lax.rem(lax.div(ids_all[0, core, s], YS), XS)
             o = lax.rem(x - from_x + XS, XS)
             for c in range(2):
                 at = (c * 3 + s) * UNIT
@@ -204,7 +211,7 @@
 
     def unpack_keys(part, o, block):
         for u in range(6):
-            unpack(block[u * UNIT : (u + 1) * UNIT, :], kf, part * part_keys + (o * 6 + u) * HALF)
+            unpack(block[u * UNIT : (u + 1) * UNIT, :], kf, part * part_keys + (o * 6 + u) * ROWS)
 
     def products(at, count):
         keys = kb[at : at + count, :]
@@ -231,17 +238,18 @@
         gb[pl.ds(at, step), :] = jnp.where(live_rows(at), gb[pl.ds(at, step), :].astype(F32), 0.0).astype(BF16)
 
     products(node_keys, own_rows)
-    for part in range(2):
+    for part in range(PARTS):
         unpack_keys(part, 0, zs[part].astype(F32))
     pk[...] = jnp.zeros(pk.shape, F32)
-    for part in range(2):
+    for part in range(PARTS):
         for o in (1, 3, 2):
             if o < ZHI:
                 z_copy(part, o).wait_recv()
                 unpack_keys(part, o, zr[part, o].astype(F32))
-        at = part * part_keys
-        kb[at : at + part_keys, :] = kf[at : at + part_keys, :].astype(BF16)
-        products(at, part_keys)
+        if part % 2:
+            at, count = (part - 1) * part_keys, 2 * part_keys
+            kb[at : at + count, :] = kf[at : at + count, :].astype(BF16)
+            products(at, count)
 
     @pl.loop(0, 2 * half // step)
     def _(b):
@@ -272,14 +280,15 @@
             pbt[at : at + count, :], gb[...], (((1,), (0,)), ((), ())), preferred_element_type=F32
         )
 
-    for part in range(2):
-        key_terms(part * part_keys, part_keys)
+    for part in range(PARTS):
+        if part % 2 == 0:
+            key_terms(part * part_keys, 2 * part_keys)
         for o in (2, 1, 3, 0):
             if o < ZHI:
                 back = (ZHI - o) % ZHI
                 for u in range(6):
-                    at = part * part_keys + (o * 6 + u) * HALF
-                    pack(dk[at : at + HALF, :], pk.at[back, part], u * UNIT)
+                    at = part * part_keys + (o * 6 + u) * ROWS
+                    pack(dk[at : at + ROWS, :], pk.at[back, part], u * UNIT)
                 if back:
                     zs2[part, back] = pk[back, part].astype(BF16)
                     z2_copy(part, back).start()
@@ -299,12 +308,12 @@
         lane = lax.broadcasted_iota(jnp.int32, pick.shape[:1] + (128,), 1)
         line = lax.broadcasted_iota(jnp.int32, pick.shape[:1] + (128,), 0)
         goal = jnp.full(lane.shape, -1, jnp.int32)
-        for quad in range(4):
-            term = group * 4 + quad
+        for which in range(128 // UNIT):
+            term = group * (128 // UNIT) + which
             o, c, s = term // 6, (term // 3) % 2, term % 3
             node = ids_all[o, lax.rem(core + c, 2), s]
-            place_ = jnp.where((node // YS) % XS == x, column_of(node), -1)
-            goal = jnp.where(lane // UNIT == quad, place_, goal)
+            place_ = jnp.where(lax.rem(lax.div(node, YS), XS) == x, column_of(node), -1)
+            goal = jnp.where(lane // UNIT == which, place_, goal)
         hit = (line // UNIT == goal) & (line % UNIT == lane % UNIT)
         pick[:, group * 128 : (group + 1) * 128] = jnp.where(hit, 1.0, 0.0).astype(BF16)
 
@@ -324,7 +333,7 @@
     def x2_copy(part, o, c):
         return remote(xs2.at[part, c], xr2.at[part, o, c], sem_x2, (part, o, c), x_peer(o, c))
 
-    for part in range(2):
+    def sum_over_z(part):
         total = pk[0, part]
         for o in range(1, ZHI):
             z2_copy(part, o).wait_recv()
@@ -339,6 +348,23 @@
     def ag_copy(o):
         return remote(ag.at[0], ag.at[o], sem_ag, (o,), z_peer(o))
 
+    def y2_copy(part, k):
+        a, b = column_place(k, 1)
+        return remote(ys.at[part, a * YS + b], yr.at[part, k], sem_y2, (part, k), column_peer(k))
+
+    def sum_over_x(part):
+        for o, c in x_moves:
+            x2_copy(part, o, c).wait_recv()
+        terms = xr2[part].reshape(XS * 2 * 3 * UNIT, 128)
+        sums = jnp.dot(pick[...], terms, preferred_element_type=F32)
+        ys[part] = sums.astype(BF16).reshape(columns, UNIT, 128)
+        for k in range(columns - 1):
+            y2_copy(part, k).start()
+
+    for part in range(PARTS - 1):
+        sum_over_z(part)
+    sum_over_x(0)
+    sum_over_z(PARTS - 1)
     at = pl.multiple_of(node_keys + zhi * quarter, quarter)
     total = dk[pl.ds(at, quarter), :]
     for o in range(1, ZHI):
@@ -348,20 +374,8 @@
     for o in range(1, ZHI):
         ag_copy(o).start()
 
-    def y2_copy(part, k):
-        a, b = column_place(k, 1)
-        return remote(ys.at[part, a * YS + b], yr.at[part, k], sem_y2, (part, k), column_peer(k))
-
-    for part in range(2):
-        for o, c in x_moves:
-            x2_copy(part, o, c).wait_recv()
-        terms = xr2[part].reshape(XS * 2 * 3 * UNIT, 128)
-        sums = jnp.dot(pick[...], terms, preferred_element_type=F32)
-        ys[part] = sums.astype(BF16).reshape(columns, UNIT, 128)
-
-        @pl.loop(0, columns - 1)
-        def _(k):
-            y2_copy(part, k).start()
+    for part in range(1, PARTS):
+        sum_over_x(part)
 
     for o in range(1, ZHI):
         ag_copy(o).wait_recv()
@@ -371,10 +385,8 @@
     fin = remote(own_out.at[core], own_out.at[core], sem_fin, (), x_peer(0, 1))
     fin.start()
 
-    for part in range(2):
-
-        @pl.loop(0, columns - 1)
-        def _(k):
+    for part in range(PARTS):
+        for k in range(columns - 1):
             y_copy(part, k).wait_send()
 
         for o, c in x_moves:
@@ -389,19 +401,17 @@
     att_local.wait()
     att_swap.wait()
 
-    for part in range(2):
+    for part in range(PARTS):
         for k in range(columns - 1):
             y2_copy(part, k).wait_recv()
         total = ys[part, mine].astype(F32)
         for k in range(columns - 1):
             total = total + yr[part, k].astype(F32)
-        unpack(total, dk, part * HALF)
+        unpack(total, dk, part * ROWS)
     node_out[...] = dk[0:SLICE, :].astype(BF16)
     fin.wait()
-    for part in range(2):
-
-        @pl.loop(0, columns - 1)
-        def _(k):
+    for part in range(PARTS):
+        for k in range(columns - 1):
             y2_copy(part, k).wait_send()
 
 
@@ -413,7 +423,6 @@
     keys = node_keys + own_rows
     columns = ZLO * YS
     vmem = pl.BlockSpec(memory_space=pltpu.VMEM)
-    smem = pl.BlockSpec(memory_space=pltpu.SMEM)
     hbm = pl.BlockSpec(memory_space=pl.ANY)
     dma = pltpu.SemaphoreType.DMA
     flops = 2 * total * keys * (3 * LAT + 2 * LATW)
@@ -424,7 +433,7 @@
             pltpu.VMEM((SLICE, width), BF16),
             pltpu.VMEM((2, own_rows, width), BF16),
         ),
-        in_specs=[hbm, hbm, hbm, hbm, hbm, smem, smem],
+        in_specs=[hbm, hbm, hbm, hbm, hbm, hbm],
         out_specs=(hbm, vmem, vmem),
         scratch_shapes=[
             pltpu.VMEM((heads, width, rows), BF16),
@@ -440,38 +449,38 @@
             pltpu.VMEM((keys, total), F32),
             pltpu.VMEM((keys, total), F32),
             pltpu.VMEM((keys, width), F32),
-            pltpu.VMEM((ZHI, 2, 6 * UNIT, 128), F32),
+            pltpu.VMEM((ZHI, PARTS, 6 * UNIT, 128), F32),
             pltpu.VMEM((keys, total), BF16),
             pltpu.VMEM((keys, total), BF16),
             pltpu.VMEM((total, LAT), BF16),
             pltpu.SMEM((XS, 2, 3), jnp.int32),
+            pltpu.SMEM((XS, 2, 3), jnp.int32),
+            pltpu.SMEM((2,), jnp.int32),
             pltpu.VMEM((columns * UNIT, XS * 6 * UNIT), BF16),
-            pltpu.VMEM((columns, UNIT, 128), BF16),
-            pltpu.VMEM((columns, UNIT, 128), BF16),
-            pltpu.VMEM((2, XS, 2, 3 * UNIT, 128), BF16),
-            pltpu.VMEM((XS, 2, 3 * UNIT, 128), BF16),
-            pltpu.VMEM((XS, 2, 3 * UNIT, 128), BF16),
-            pltpu.VMEM((2, 6 * UNIT, 128), BF16),
-            pltpu.VMEM((2, ZHI, 6 * UNIT, 128), BF16),
-            pltpu.VMEM((2, ZHI, 6 * UNIT, 128), BF16),
-            pltpu.VMEM((2, ZHI, 6 * UNIT, 128), BF16),
-            pltpu.VMEM((2, 2, 3 * UNIT, 128), BF16),
-            pltpu.VMEM((2, XS, 2, 3 * UNIT, 128), BF16),
-            pltpu.VMEM((2, columns, UNIT, 128), BF16),
-            pltpu.VMEM((2, columns, UNIT, 128), BF16),
+            [pltpu.VMEM((columns, UNIT, 128), BF16)] * PARTS,
+            pltpu.VMEM((PARTS, XS, 2, 3 * UNIT, 128), BF16),
+            [pltpu.VMEM((XS, 2, 3 * UNIT, 128), BF16)] * PARTS,
+            pltpu.VMEM((PARTS, 6 * UNIT, 128), BF16),
+            pltpu.VMEM((PARTS, ZHI, 6 * UNIT, 128), BF16),
+            pltpu.VMEM((PARTS, ZHI, 6 * UNIT, 128), BF16),
+            pltpu.VMEM((PARTS, ZHI, 6 * UNIT, 128), BF16),
+            pltpu.VMEM((PARTS, 2, 3 * UNIT, 128), BF16),
+            pltpu.VMEM((PARTS, XS, 2, 3 * UNIT, 128), BF16),
+            pltpu.VMEM((PARTS, columns, UNIT, 128), BF16),
+            pltpu.VMEM((PARTS, columns, UNIT, 128), BF16),
             pltpu.VMEM((ZHI, own_rows // ZHI, width), BF16),
             pltpu.VMEM((ZHI, own_rows // ZHI, width), BF16),
             pltpu.VMEM((ZHI, own_rows // ZHI, width), BF16),
-            dma((5,)),
+            dma((7,)),
             dma((2, 2)),
             dma((2,)),
             dma((2, XS)),
-            dma((2, 2, columns)),
-            dma((2, 2, XS, 2)),
-            dma((2, 2, ZHI)),
-            dma((2, 2, ZHI)),
-            dma((2, 2, XS, 2)),
-            dma((2, 2, columns)),
+            dma((2, PARTS, columns)),
+            dma((2, PARTS, XS, 2)),
+            dma((2, PARTS, ZHI)),
+            dma((2, PARTS, ZHI)),
+            dma((2, PARTS, XS, 2)),
+            dma((2, PARTS, columns)),
             dma((2, ZHI)),
             dma((2, ZHI)),
             dma((2,)),
@@ -489,7 +498,6 @@
         leaf_latent.T,
         leaf_nodes,
         node_latent.reshape(SLICE, width),
-        leaf_nodes,
         leaf_lengths,
     )
     return (

time: 70 us -> 68.7 us (0.981)
  Pallas kernels: 66.8 us -> 65.5 us
    pallas_call x1, Pallas kernels: 66.8 us -> 65.5 us  [body(): pl.pallas_call(kernel, out_shape=(pltpu.VMEM((total, LAT), BF16), pltpu.V...]
where the time goes in v3:
time: 68.7 us; the launch traced here: 68.5 us
  Pallas kernels  65.5 us (95%)
  local copies, waits for them, and re-layouts  2.37 us (3%)
    pallas_call x1, Pallas kernels, body(): pl.pallas_call(kernel, out_shape=(pltpu.VMEM((total, LAT), BF16), pltpu.V...  65.5 us
    unnamed x3, local copies, waits for them, and re-layouts  2.37 us

profile of v3, /device:TPU:1, one launch (start us, length us, event | category | flops | bytes accessed | tf_op | source)
XLA Modules:
  0.0 68.5 jit_solution(17786896140653674227)
XLA Ops:
  0.6 65.5 %leaves.1 = (bf16[1024,512]{1,0:T(8,128)(2,1)S(1)}, bf16[12,576]{1,0:T(8,128)(2,1)S(1)}, bf16[2,64,576]{2,1,0:T(8,128)(2,1)S(1)}) custom-call(bf16[8,576,128]{2,1,0:T(8,128)(2,1)} %bitcast.10, bf16[1024,512]{1,0:T(8,128)(2,1)} %bitcast.11, bf16[576,128]{1,0:T(8,128)(2,1)} %bitcast.12, s32[2,3]{1,0:T(2,128)} %ids_hbm.1, bf16[12,576]{1,0:T(8,128)(2,1)} %bitcast.13, ...), custom_call_target="tpu_custom_call" | custom-call | flops 1937768448 | bytes 3276800 | tf_op jit(solution)/shard_map/leaves/pallas_call | solution.py:429
  66.2 1.0 %copy.12 = bf16[128,8,512]{2,1,0:T(8,128)(2,1)} copy(bf16[128,8,512]{2,1,0:T(8,128)(2,1)S(1)} %bitcast.7) | data formatting | bytes 2097152
  67.1 0.6 copy.13
  67.7 0.8 %copy.9 = bf16[128,576]{0,1:T(8,128)(2,1)} copy(bf16[128,576]{1,0:T(8,128)(2,1)S(1)} %bitcast.9) | data formatting | bytes 294912
